TPU v7x, 256 devices: a whole 4x4x8 slice. The times are simulated.
256 devices in a mesh: dp: 4 (over y), bank: 64 (over z, x, core).
Axes of the slice: x: 4, y: 4, z: 8, core: 2. Of those that a mesh axis runs over, the one named last changes fastest.
Arguments:
- region_codes: bfloat16 [2048, 1024], P(('dp', 'bank')), parts along dimension 0
- block_exponents: int32 [2048, 32], P(('dp', 'bank')), parts along dimension 0, may hold values from -3 to 2
- text_bank: bfloat16 [262144, 1024], P('bank')
Outputs:
- expected: bfloat16 [2048, 1024], P(('dp', 'bank')), parts along dimension 0
There are 4 independent parts, one for each index of `dp`. A program takes and returns all parts, laid end to end along the dimension named above; an argument that names none is the same for every part. Nothing has to cross between parts.
All inputs are finite; a program needn't handle non-finite values.
Results may differ from a plain program's by a relative error of at most 0.003.
Values may be sent and summed in bfloat16 or wider, within the bound.
A program may use at most 320 MiB of HBM per device.

v0:
```python
import jax
import jax.numpy as jnp
from jax import lax
from jax.sharding import PartitionSpec as P

logit_scale = 2.0


def dequantize(codes, exponents):
    expanded = jnp.repeat(jnp.exp2(exponents.astype(jnp.float32)), 32, axis=1)
    return (codes.astype(jnp.float32) * expanded).astype(jnp.bfloat16)


def local(region_codes, block_exponents, text_bank):
    regions = dequantize(region_codes, block_exponents)
    logits = logit_scale * lax.dot_general(
        lax.all_gather(regions, "bank", axis=0, tiled=True),
        text_bank,
        (((1,), (1,)), ((), ())),
        preferred_element_type=jnp.float32,
    )
    peaks = jnp.max(logits, axis=1)
    shifted = jnp.exp(logits - peaks[:, None])
    totals = jnp.sum(shifted, axis=1)
    partial_value = jnp.dot(
        shifted.astype(jnp.bfloat16), text_bank, preferred_element_type=jnp.float32
    )
    rows_here = region_codes.shape[0]
    offset = lax.axis_index("bank") * rows_here
    highest = lax.pmax(peaks, "bank")
    factor = jnp.exp(peaks - highest)
    scaled = partial_value * factor[:, None]
    weighted_totals = totals * factor
    all_totals = lax.psum(weighted_totals, "bank")
    numerator = lax.psum_scatter(scaled, "bank", scatter_dimension=0, tiled=True)
    denominator = lax.dynamic_slice_in_dim(all_totals, offset, rows_here, 0)
    return (numerator / denominator[:, None]).astype(jnp.bfloat16)


def solution(mesh):
    return jax.shard_map(
        local,
        mesh=mesh,
        in_specs=(P(("dp", "bank"), None), P(("dp", "bank"), None), P("bank", None)),
        out_specs=P(("dp", "bank"), None),
        check_vma=False,
    )
```

profile of v0, /device:TPU:16, one launch (start us, length us, event | category | flops | bytes accessed | tf_op | source)
XLA Modules:
  0.0 438.0 jit_solution(5726463222699489783)
XLA Ops:
  6.5 0.0 all-gather.2.cloned.1.call-start
  6.5 0.7 multiply_exponential_fusion
  7.2 0.1 broadcast_in_dim.2
  7.3 0.1 reshape.6
  7.4 1.3 multiply_convert_fusion
  8.8 0.0 all-gather.2.cloned.1.call-update
  8.8 0.0 all-reduce.3.cloned.1.call-start
  8.8 80.4 %all-gather.2.cloned.1.call-done = bf16[512,1024]{1,0:T(8,128)(2,1)} async-done(((bf16[8,1024]{1,0:T(8,128)(2,1)}), bf16[512,1024]{1,0:T(8,128)(2,1)}) %all-gather.2.cloned.1.call-update) | async-done | bytes 1048592 | tf_op jit(solution)/shard_map/all_gather | solution.py:17
  89.3 11.5 %multiply_reduce_fusion = (f32[512]{0:T(512)S(1)}, f32[512,4096]{1,0:T(8,128)}) fusion(bf16[512,1024]{1,0:T(8,128)(2,1)} %all-gather.2.cloned.1.call-done, bf16[4096,1024]{1,0:T(8,128)(2,1)} %param.5), kind=kOutput, calls=%fused_computation.1 | convolution fusion | flops 4299161088 | bytes 17827840 | tf_op jit(solution)/shard_map/dot_general | solution.py:16
  100.7 126.5 %pmax.7 = f32[512]{0:T(512)S(1)} all-reduce(f32[512]{0:T(512)S(1)} %get-tuple-element.7), channel_id=1, replica_groups=mesh['dp'=4,'bank'=64] {'bank'}, use_global_device_ids=true, to_apply=%region_1.0 | all-reduce | flops 512 | bytes 4096 | tf_op jit(solution)/shard_map/pmax | solution.py:30
  227.3 0.0 copy-start
  227.3 5.0 %fusion = f32[512]{0:T(512)S(1)} fusion(f32[512,4096]{1,0:T(8,128)} %get-tuple-element.8, f32[512]{0:T(512)S(1)} %get-tuple-element.7), kind=kLoop, calls=%fused_computation.2 | loop fusion | flops 6290944 | bytes 8392704 | tf_op jit(solution)/shard_map/reduce_sum | solution.py:24
  232.3 0.7 copy-done
  233.0 0.0 copy-start.1
  233.0 9.3 %fusion.6 = f32[512,1024]{1,0:T(8,128)} fusion(bf16[4096,1024]{1,0:T(8,128)(2,1)} %param.5, f32[512,4096]{1,0:T(8,128)S(1)} %copy-done, f32[512]{0:T(512)S(1)} %get-tuple-element.7, f32[512]{0:T(512)S(1)} %get-tuple-element.6), kind=kOutput, calls=%fused_computation.7 | convolution fusion | flops 4301783040 | bytes 18878464 | tf_op jit(solution)/shard_map/dot_general | solution.py:25
  242.4 0.0 all-reduce.3.cloned.1.call-update
  242.4 0.0 copy-done.1
  242.4 0.6 dynamic-slice
  243.6 124.3 %psum.7 = f32[512]{0:T(512)S(1)} all-reduce(f32[512]{0:T(512)S(1)} %get-tuple-element.5), channel_id=1, replica_groups=mesh['dp'=4,'bank'=64] {'bank'}, use_global_device_ids=true, to_apply=%region_4.0 | all-reduce | flops 512 | bytes 4096 | tf_op jit(solution)/shard_map/psum | solution.py:34
  367.9 0.1 dynamic_slice.3
  368.0 61.7 %all-reduce.3.cloned.1.call-done = f32[512,1024]{1,0:T(8,128)} async-done(((f32[512,1024]{1,0:T(8,128)}), f32[512,1024]{1,0:T(8,128)}) %all-reduce.3.cloned.1.call-update) | async-done | bytes 2097168
  429.7 1.4 fusion.9
  (1 shorter events, 0.0 us)
Async XLA Ops:
  6.5 82.7 %all-gather.2.cloned.1.call-start = ((), (), s32[]{:S(2)}) async-start(), calls=%async_computation | async-start | bytes 1064960 | tf_op jit(solution)/shard_map/all_gather | solution.py:17
  8.8 420.9 %all-reduce.3.cloned.1.call-start = ((), (), s32[]{:S(2)}) async-start(), calls=%async_computation.1 | async-start | bytes 4194304
  227.3 5.8 %copy-start = (f32[512,4096]{1,0:T(8,128)S(1)}, f32[512,4096]{1,0:T(8,128)}, u32[]{:S(2)}) copy-start(f32[512,4096]{1,0:T(8,128)} %get-tuple-element.8) | copy-start | bytes 25165828
  233.0 9.4 %copy-start.1 = (u32[256]{0:T(256)S(1)}, u32[256]{0:T(256)}, u32[]{:S(2)}) copy-start(u32[256]{0:T(256)} %constant.22) | copy-start | bytes 3076
Sparse Core Ops, SparseCore 0:
  10.1 79.0 all-gather.1
  242.5 187.1 all-reduce.2
where the time goes:
time: 438 us
  blocking collectives  251 us (57%)
  waiting for transfers between devices  142 us (32%)
  matrix products  20.8 us (5%)
  between operations  14.1 us (3%)
  other arithmetic  8.49 us (2%)
    pmax x1, blocking collectives, local(): highest = lax.pmax(peaks, 'bank')  127 us
    psum x1, blocking collectives, local(): all_totals = lax.psum(weighted_totals, 'bank')  124 us
    all_gather x1, waiting for transfers between devices, local(): lax.all_gather(regions, 'bank', axis=0, tiled=True)  80.4 us
    unnamed x3, waiting for transfers between devices  61.8 us
    dot_general x1, matrix products, local(): lax.dot_general(lax.all_gather(regions, 'bank', axis=0, tiled=True), text...  11.5 us
    dot_general x1, matrix products, local(): jnp.dot(shifted.astype(jnp.bfloat16), text_bank, preferred_element_type=j...  9.35 us
  transfers between devices with their start and end apart: 2, of which 2 were waited for; matrix products, arithmetic and copies ran while one was open for 0% of the time, Pallas kernels for 0%

commit v1 on v0

v1 whole, which is shorter than its diff:
```python
import math

import jax
import jax.numpy as jnp
from jax import lax
from jax.experimental import pallas as pl
from jax.experimental.pallas import tpu as pltpu
from jax.sharding import PartitionSpec as P

MESH = pl.DeviceIdType.MESH
D = 1024
HALF = D // 2
VDEV = 4096
NZ, NX = 8, 4
OWN = 8
PLANE = 2 * NX * OWN
WIDE = D + 128
SLOTS = (0, 1, 7, 2, 6, 3, 5, 4)
FAR = (4, 3, 5, 2, 6, 1, 7)
CHUNK = 2 * PLANE
NCHUNK = NZ // 2
LOADS = 8
QTILE = 1024
SCALE = 2.0 / math.log(2.0)


def merge(parts):
    top = parts[0][0]
    for m, _, _ in parts[1:]:
        top = jnp.maximum(top, m)
    total, rows = None, None
    for m, s, p in parts:
        f = jnp.exp2((m - top) * SCALE)
        total = s * f if total is None else total + s * f
        rows = p * f if rows is None else rows + p * f
    return top, total, rows


def pack_ms(m, s):
    lane = lax.broadcasted_iota(jnp.int32, (m.shape[0], 128), 1)
    return jnp.where(lane < 64, m, s)


def unpack_ms(tile):
    return tile[:, 0:1], tile[:, 64:65]


def to_travel(rows):
    return jnp.concatenate([rows[:, :HALF], rows[:, HALF:]], axis=0)


def from_travel(block):
    return jnp.concatenate([block[:OWN], block[OWN:]], axis=1)


def kernel(
    codes_ref, exps_ref, text_hbm, out_ref,
    text, gath, regs, logit, wgt, pbuf, cbuf, xsend, xsms, xb, xbms, qown, zsend, zb,
    load_sem, gz_s, gz_r, gx_s, gx_r, gc_s, gc_r, rc_s, rc_r, rx_s, rx_r, rm_s, rm_r, rz_s, rz_r,
):
    me = lax.axis_index("bank")
    z, x, c = me // (2 * NX), (me // 2) % NX, me % 2

    def at(dz, dx, dc):
        return {"bank": ((z + dz) % NZ) * (2 * NX) + ((x + dx) % NX) * 2 + (c + dc) % 2}

    def remote(src, dst, s, r, dev):
        return pltpu.make_async_remote_copy(
            src_ref=src, dst_ref=dst, send_sem=s, recv_sem=r, device_id=dev, device_id_type=MESH
        )

    span = VDEV // LOADS
    loads = [
        pltpu.make_async_copy(
            text_hbm.at[pl.ds(k * span, span)], text.at[pl.ds(k * span, span)], load_sem.at[k]
        )
        for k in range(LOADS)
    ]
    for ld in loads:
        ld.start()

    scale = jnp.exp2(exps_ref[...].astype(jnp.float32)).astype(jnp.bfloat16)
    feat = lax.broadcasted_iota(jnp.int32, (32, D), 1) // 32
    blk = lax.broadcasted_iota(jnp.int32, (32, D), 0)
    spread = jnp.where(feat == blk, 1.0, 0.0).astype(jnp.bfloat16)
    expanded = jnp.dot(scale, spread, preferred_element_type=jnp.float32)
    own = codes_ref[...].astype(jnp.float32) * expanded
    gath[0, 0, 0] = to_travel(own).astype(jnp.bfloat16)

    barrier = pltpu.get_barrier_semaphore()
    peers = [at(d, 0, 0) for d in FAR] + [at(0, i, 0) for i in (2, 1, 3)] + [at(0, 0, 1)]
    for p in peers:
        pl.semaphore_signal(barrier, inc=1, device_id=p, device_id_type=MESH)
    pl.semaphore_wait(barrier, len(peers))

    started = []

    def go(copy):
        copy.start()
        started.append(copy)
        return copy

    gz = {}
    for e in FAR:
        d = (NZ - e) % NZ
        gz[d] = go(remote(gath.at[0, 0, 0], gath.at[d, 0, 0], gz_s.at[d], gz_r.at[d], at(e, 0, 0)))
    gx = {}

    def forward(d):
        for i in (2, 1, 3):
            j = NX - i
            gx[d, j] = go(remote(gath.at[d, 0, 0], gath.at[d, 0, j], gx_s.at[d, j], gx_r.at[d, j], at(0, i, 0)))

    gc = {}

    def swap(d):
        for j in (1, 2, 3):
            gx[d, j].wait_recv()
        gc[d] = go(remote(gath.at[d, 0], gath.at[d, 1], gc_s.at[d], gc_r.at[d], at(0, 0, 1)))

    forward(0)
    for d in SLOTS[1:]:
        gz[d].wait_recv()
        forward(d)
    for slot, d in enumerate(SLOTS):
        swap(d)
    for slot, d in enumerate(SLOTS):
        gc[d].wait_recv()
        for cr in range(2):
            for i in range(0, NX, 2):
                a = from_travel(gath[d, cr, i].astype(jnp.float32))
                b = from_travel(gath[d, cr, i + 1].astype(jnp.float32))
                r0 = slot * PLANE + cr * (NX * OWN) + i * OWN
                regs[r0 : r0 + 2 * OWN, :] = jnp.concatenate([a, b], axis=0).astype(jnp.bfloat16)
    for ld in loads:
        ld.wait()

    n = NZ * PLANE
    peak = jnp.full((n, 128), -jnp.inf, jnp.float32)
    for t in range(VDEV // QTILE):
        dots = lax.dot_general(
            regs[...], text[t * QTILE : (t + 1) * QTILE, :], (((1,), (1,)), ((), ())),
            preferred_element_type=jnp.float32,
        )
        logit[:, t * QTILE : (t + 1) * QTILE] = dots
        for q in range(QTILE // 128):
            peak = jnp.maximum(peak, dots[:, q * 128 : (q + 1) * 128])
    top = jnp.max(peak, axis=1, keepdims=True)

    rc, rx, rm, rz = {}, {}, {}, {}
    order = list(range(NCHUNK - 1, -1, -1))

    def weights(g):
        lo = g * CHUNK
        m = top[lo : lo + CHUNK]
        total = jnp.zeros((CHUNK, 128), jnp.float32)
        for k in range(VDEV // 128):
            e = jnp.exp2((logit[lo : lo + CHUNK, k * 128 : (k + 1) * 128] - m) * SCALE)
            total = total + e
            wgt[lo : lo + CHUNK, k * 128 : (k + 1) * 128] = e.astype(jnp.bfloat16)
        s = jnp.sum(total, axis=1, keepdims=True)
        pbuf[lo : lo + CHUNK, D:] = pack_ms(m, s)

    def values(g):
        lo = g * CHUNK
        for k in range(2):
            pbuf[lo : lo + CHUNK, k * HALF : (k + 1) * HALF] = jnp.dot(
                wgt[lo : lo + CHUNK, :], text[:, k * HALF : (k + 1) * HALF], preferred_element_type=jnp.float32
            )
        for slot in (2 * g + 1, 2 * g):
            rc[slot] = go(remote(
                pbuf.at[pl.ds(slot * PLANE + NX * OWN, NX * OWN)], cbuf.at[slot],
                rc_s.at[slot], rc_r.at[slot], at(0, 0, 1),
            ))

    def pair_sum(slot):
        rc[slot].wait_recv()
        lo = slot * PLANE
        a = pbuf[lo : lo + NX * OWN, :]
        b = cbuf[slot]
        m, s, p = merge([(*unpack_ms(a[:, D:]), a[:, :D]), (*unpack_ms(b[:, D:]), b[:, :D])])
        ms = pack_ms(m, s)
        qown[slot, :, :D] = p[:OWN]
        qown[slot, :, D:] = ms[:OWN]
        for i in (2, 1, 3):
            j = NX - i
            xsend[slot, i] = to_travel(p[i * OWN : (i + 1) * OWN]).astype(jnp.bfloat16)
            xsms[slot, i] = ms[i * OWN : (i + 1) * OWN]
            rx[slot, j] = go(remote(xsend.at[slot, i], xb.at[slot, j], rx_s.at[slot, i], rx_r.at[slot, j], at(0, i, 0)))
            rm[slot, j] = go(remote(xsms.at[slot, i], xbms.at[slot, j], rm_s.at[slot, i], rm_r.at[slot, j], at(0, i, 0)))

    def x_sum(slot):
        d = SLOTS[slot]
        own_part = qown[slot]
        parts = [(*unpack_ms(own_part[:, D:]), own_part[:, :D])]
        for j in (1, 2, 3):
            rx[slot, j].wait_recv()
            rm[slot, j].wait_recv()
            parts.append((*unpack_ms(xbms[slot, j]), from_travel(xb[slot, j].astype(jnp.float32))))
        m, s, p = merge(parts)
        if d == 0:
            zb[0, :, :D] = p
            zb[0, :, D:] = pack_ms(m, s)
            return
        zsend[slot, :, :D] = p
        zsend[slot, :, D:] = pack_ms(m, s)
        e = (NZ - d) % NZ
        rz[e] = go(remote(zsend.at[slot], zb.at[e], rz_s.at[e], rz_r.at[e], at(d, 0, 0)))

    weights(order[0])
    for n_, g in enumerate(order):
        values(g)
        if n_ + 1 < NCHUNK:
            weights(order[n_ + 1])
        if n_ >= 2:
            for slot in (2 * order[n_ - 2] + 1, 2 * order[n_ - 2]):
                x_sum(slot)
        if n_ >= 1:
            for slot in (2 * order[n_ - 1] + 1, 2 * order[n_ - 1]):
                pair_sum(slot)
    last = order[-1]
    for slot in (2 * last + 1, 2 * last):
        pair_sum(slot)
    for g in order[-2:]:
        for slot in (2 * g + 1, 2 * g):
            x_sum(slot)

    parts = []
    for d in range(NZ):
        if d:
            rz[d].wait_recv()
        parts.append((*unpack_ms(zb[d, :, D:]), zb[d, :, :D]))
    m, s, p = merge(parts)
    out_ref[...] = (p / s).astype(jnp.bfloat16)
    for cp in started:
        cp.wait_send()


def local(codes, exps, text_bank):
    dma = pltpu.SemaphoreType.DMA
    f32, bf16 = jnp.float32, jnp.bfloat16
    n = NZ * PLANE
    return pl.pallas_call(
        kernel,
        out_shape=jax.ShapeDtypeStruct((OWN, D), bf16),
        in_specs=[
            pl.BlockSpec(memory_space=pltpu.VMEM),
            pl.BlockSpec(memory_space=pltpu.VMEM),
            pl.BlockSpec(memory_space=pl.ANY),
        ],
        out_specs=pl.BlockSpec(memory_space=pltpu.VMEM),
        scratch_shapes=[
            pltpu.VMEM((VDEV, D), bf16),
            pltpu.VMEM((NZ, 2, NX, 2 * OWN, HALF), bf16),
            pltpu.VMEM((n, D), bf16),
            pltpu.VMEM((n, VDEV), f32),
            pltpu.VMEM((n, VDEV), bf16),
            pltpu.VMEM((n, WIDE), f32),
            pltpu.VMEM((NZ, NX * OWN, WIDE), f32),
            pltpu.VMEM((NZ, NX, 2 * OWN, HALF), bf16),
            pltpu.VMEM((NZ, NX, OWN, 128), f32),
            pltpu.VMEM((NZ, NX, 2 * OWN, HALF), bf16),
            pltpu.VMEM((NZ, NX, OWN, 128), f32),
            pltpu.VMEM((NZ, OWN, WIDE), f32),
            pltpu.VMEM((NZ, OWN, WIDE), f32),
            pltpu.VMEM((NZ, OWN, WIDE), f32),
            dma((LOADS,)),
            dma((NZ,)), dma((NZ,)),
            dma((NZ, NX)), dma((NZ, NX)),
            dma((NZ,)), dma((NZ,)),
            dma((NZ,)), dma((NZ,)),
            dma((NZ, NX)), dma((NZ, NX)),
            dma((NZ, NX)), dma((NZ, NX)),
            dma((NZ,)), dma((NZ,)),
        ],
        compiler_params=pltpu.CompilerParams(
            collective_id=0, has_side_effects=True, vmem_limit_bytes=48 * 2**20
        ),
    )(codes, exps, text_bank)


def solution(mesh):
    return jax.shard_map(
        local,
        mesh=mesh,
        in_specs=(P(("dp", "bank"), None), P(("dp", "bank"), None), P("bank", None)),
        out_specs=P(("dp", "bank"), None),
        check_vma=False,
    )
```

time: 438 us -> 51.1 us (0.12)
  blocking collectives: 251 us -> 0 us
  waiting for transfers between devices: 142 us -> 0 us
  Pallas kernels: 0 us -> 48.9 us
  matrix products: 20.8 us -> 0 us
  between operations: 14.1 us -> 0.01 us
  other arithmetic: 8.49 us -> 0 us
    pmax x1 -> x0, blocking collectives: 127 us -> none  [local(): highest = lax.pmax(peaks, 'bank')]
    psum x1 -> x0, blocking collectives: 124 us -> none  [local(): all_totals = lax.psum(weighted_totals, 'bank')]
    all_gather x1 -> x0, waiting for transfers between devices: 80.4 us -> none  [local(): lax.all_gather(regions, 'bank', axis=0, tiled=True)]
    unnamed x3 -> x0, waiting for transfers between devices: 61.8 us -> none
    pallas_call x0 -> x1, Pallas kernels: none -> 48.9 us  [local(): pl.pallas_call(kernel, out_shape=jax.ShapeDtypeStruct((OWN, D), bf16), in...]
    dot_general x2 -> x0, matrix products: 20.8 us -> none  [the longest x1 11.5 us: local(): lax.dot_general(lax.all_gather(regions, 'bank', axis=0, tiled=True), text...]
    reduce_sum x1 -> x0, other arithmetic: 5.02 us -> none  [local(): totals = jnp.sum(shifted, axis=1)]
  transfers between devices with their start and end apart: 2 -> 0, of which waited for: 2 -> 0; matrix products, arithmetic and copies ran while one was open for 0% -> 0% of each run, Pallas kernels for 0% -> 0%
where the time goes in v1:
time: 51.1 us; the launch traced here: 50.9 us
  Pallas kernels  48.9 us (96%)
  local copies, waits for them, and re-layouts  2.01 us (4%)
    pallas_call x1, Pallas kernels, local(): pl.pallas_call(kernel, out_shape=jax.ShapeDtypeStruct((OWN, D), bf16), in...  48.9 us
    unnamed x5, local copies, waits for them, and re-layouts  2.01 us

profile of v1, /device:TPU:16, one launch (start us, length us, event | category | flops | bytes accessed | tf_op | source)
XLA Modules:
  0.0 50.9 jit_solution(8983100172627087524)
XLA Ops:
  0.0 0.0 copy-start
  0.0 0.7 %copy-done = bf16[8,1024]{1,0:T(8,128)(2,1)S(1)} copy-done((bf16[8,1024]{1,0:T(8,128)(2,1)S(1)}, bf16[8,1024]{1,0:T(8,128)(2,1)}, u32[]{:S(2)}) %copy-start) | copy-done | bytes 16408
  0.7 0.0 copy-start.1
  0.7 0.7 %copy-done.1 = s32[8,32]{1,0:T(8,128)S(1)} copy-done((s32[8,32]{1,0:T(8,128)S(1)}, s32[8,32]{1,0:T(8,128)}, u32[]{:S(2)}) %copy-start.1) | copy-done | bytes 1048
  1.4 48.9 %shard_map.37 = bf16[8,1024]{1,0:T(8,128)(2,1)S(1)} custom-call(bf16[8,1024]{1,0:T(8,128)(2,1)S(1)} %copy-done, s32[8,32]{1,0:T(8,128)S(1)} %copy-done.1, bf16[4096,1024]{1,0:T(8,128)(2,1)} %text_hbm.1), custom_call_target="tpu_custom_call" | custom-call | tf_op jit(solution)/shard_map/pallas_call | solution.py:243
  50.3 0.6 %copy.5 = bf16[8,1024]{1,0:T(8,128)(2,1)} copy(bf16[8,1024]{1,0:T(8,128)(2,1)S(1)} %shard_map.37) | data formatting | bytes 32768
Async XLA Ops:
  0.0 0.7 %copy-start = (bf16[8,1024]{1,0:T(8,128)(2,1)S(1)}, bf16[8,1024]{1,0:T(8,128)(2,1)}, u32[]{:S(2)}) copy-start(bf16[8,1024]{1,0:T(8,128)(2,1)} %codes_ref.1) | copy-start | bytes 49156
  0.7 0.7 %copy-start.1 = (s32[8,32]{1,0:T(8,128)S(1)}, s32[8,32]{1,0:T(8,128)}, u32[]{:S(2)}) copy-start(s32[8,32]{1,0:T(8,128)} %exps_ref.1) | copy-start | bytes 3076

commit v2 on v1

v2 whole, which is shorter than its diff:
```python
import math

import jax
import jax.numpy as jnp
from jax import lax
from jax.experimental import pallas as pl
from jax.experimental.pallas import tpu as pltpu
from jax.sharding import PartitionSpec as P

MESH = pl.DeviceIdType.MESH
D = 1024
HALF = D // 2
VDEV = 4096
NZ, NX = 8, 4
OWN = 8
PAIR = NX * OWN
PLANE = 2 * PAIR
WIDE = D + 128
MSG = HALF + 128
SLOTS = (0, 1, 7, 2, 6, 3, 5, 4)
CHUNK = 2 * PLANE
NCHUNK = NZ // 2
LOADS = 8
QTILE = 512
DIRECT_IN = (0, 1, 7)
DIRECT_OUT = (0, 1, 7)
BUNDLE_IN = (2, 6)
SENDS = (
    (0, 2), (0, 1), (0, 3), (4, 0), (3, 0), (5, 0), (1, 2), (1, 1), (1, 3), (1, 0), (7, 2), (7, 1), (7, 3), (7,
    0),
)
STEPS = (
    ("t", 0), ("t", 1), ("t", 2), ("t", 3), ("t", 4), ("t", 5), ("t", 6), ("t", 7), ("swap", 0), ("bundle", 2),
    ("bundle", 6), ("fwd", 3), ("fwd", 5), ("fwd", 4), ("swap", 1), ("swap", 7), ("pack", 0), ("pack", 1), ("q",
    0), ("swap", 3), ("swap", 5), ("swap", 4), ("swap", 2), ("swap", 6), ("pack", 6), ("pack", 7), ("q", 3),
    ("w", 0), ("pack", 4), ("pack", 5), ("q", 2), ("w", 3), ("v", 3), ("w", 2), ("give", 3), ("pack", 2),
    ("pack", 3), ("q", 1), ("v", 2), ("w", 1), ("give", 2), ("pair", 7), ("pair", 6), ("v", 1), ("give", 1),
    ("pair", 5), ("pair", 4), ("v", 0), ("give", 0), ("x", 7), ("x", 6), ("pair", 3), ("pair", 2), ("x", 5),
    ("x", 4), ("pair", 1), ("pair", 0), ("x", 3), ("end", 0), ("end", 1), ("end", 7), ("end", 6), ("end", 2),
    ("end", 3), ("end", 5), ("end", 4),
)
SCALE = 2.0 / math.log(2.0)


def merge(parts):
    top = parts[0][0]
    for m, _, _ in parts[1:]:
        top = jnp.maximum(top, m)
    total, rows = None, None
    for m, s, p in parts:
        f = jnp.exp2((m - top) * SCALE)
        total = s * f if total is None else total + s * f
        rows = p * f if rows is None else rows + p * f
    return top, total, rows


def pack_ms(m, s):
    lane = lax.broadcasted_iota(jnp.int32, (m.shape[0], 128), 1)
    return jnp.where(lane < 64, m, s)


def unpack(wide):
    return wide[:, D : D + 1], wide[:, D + 64 : D + 65], wide[:, :D]


def to_travel(rows):
    return jnp.concatenate([rows[:, :HALF], rows[:, HALF:]], axis=0)


def from_travel(block):
    return jnp.concatenate([block[:OWN], block[OWN:]], axis=1)


def to_message(m, s, rows):
    col = jnp.broadcast_to(jnp.concatenate([m, s], axis=0), (2 * OWN, 128))
    hi = col.astype(jnp.bfloat16).astype(jnp.float32)
    mid = (col - hi).astype(jnp.bfloat16).astype(jnp.float32)
    low = (col - hi) - mid
    lane = lax.broadcasted_iota(jnp.int32, col.shape, 1)
    tail = jnp.where(lane < 32, hi, jnp.where(lane < 64, mid, low))
    return jnp.concatenate([to_travel(rows), tail], axis=1).astype(jnp.bfloat16)


def from_message(block):
    wide = block.astype(jnp.float32)
    tail = wide[:, HALF:]
    col = (tail[:, 0:1] + tail[:, 32:33]) + tail[:, 64:65]
    return col[:OWN], col[OWN:], from_travel(wide[:, :HALF])


def kernel(
    codes_hbm, exps_hbm, text_hbm, out_ref,
    codes, exps, text, textt, gath, regs, logit, wgt, pbuf, cbuf, xsend, xb, qown, zsend, zb,
    load_sem, in_sem, gx_s, gx_r, gc_s, gc_r, rc_s, rc_r, rx_s, rx_r, rz_s, rz_r,
):
    me = lax.axis_index("bank")
    z, x, c = me // (2 * NX), (me // 2) % NX, me % 2

    def at(dz, dx, dc):
        return {"bank": ((z + dz) % NZ) * (2 * NX) + ((x + dx) % NX) * 2 + (c + dc) % 2}

    def remote(src, dst, s, r, dev):
        return pltpu.make_async_remote_copy(
            src_ref=src, dst_ref=dst, send_sem=s, recv_sem=r, device_id=dev, device_id_type=MESH
        )

    barrier = pltpu.get_barrier_semaphore()
    far = [(d, 0, 0) for d in (4, 3, 5, 2, 6)]
    near = [(d, i, 0) for d in sorted((set(DIRECT_IN) | set(DIRECT_OUT)) - {0}) for i in range(1, NX)]
    peers = far + near + [(1, 0, 0), (7, 0, 0), (0, 2, 0), (0, 1, 0), (0, 3, 0), (0, 0, 1)]
    for p in peers:
        pl.semaphore_signal(barrier, inc=1, device_id=at(*p), device_id_type=MESH)

    in_codes = pltpu.make_async_copy(codes_hbm, codes, in_sem.at[0])
    in_exps = pltpu.make_async_copy(exps_hbm, exps, in_sem.at[1])
    in_codes.start()
    in_exps.start()
    span = VDEV // LOADS
    loads = [
        pltpu.make_async_copy(
            text_hbm.at[pl.ds(k * span, span)], text.at[pl.ds(k * span, span)], load_sem.at[k]
        )
        for k in range(LOADS)
    ]
    for ld in loads:
        ld.start()

    feat = lax.broadcasted_iota(jnp.int32, (32, D), 1) // 32
    blk = lax.broadcasted_iota(jnp.int32, (32, D), 0)
    spread = jnp.where(feat == blk, 1.0, 0.0).astype(jnp.bfloat16)
    in_codes.wait()
    in_exps.wait()
    scale = jnp.exp2(exps[...].astype(jnp.float32)).astype(jnp.bfloat16)
    expanded = jnp.dot(scale, spread, preferred_element_type=jnp.float32)
    own = codes[...].astype(jnp.float32) * expanded
    gath[0, 0, 0] = to_travel(own).astype(jnp.bfloat16)
    pl.semaphore_wait(barrier, len(peers))

    started = []

    def go(copy):
        copy.start()
        started.append(copy)
        return copy

    gx, gc = {}, {}

    def send(e, i):
        d, j = (NZ - e) % NZ, (NX - i) % NX
        gx[d, j] = go(remote(gath.at[0, 0, 0], gath.at[d, 0, j], gx_s.at[d, j], gx_r.at[d, j], at(e, i, 0)))

    def forward(d):
        gx[d, 0].wait_recv()
        for i in (2, 1, 3):
            j = NX - i
            gx[d, j] = go(remote(gath.at[d, 0, 0], gath.at[d, 0, j], gx_s.at[d, j], gx_r.at[d, j], at(0, i, 0)))

    def bundle(e):
        d = (NZ - e) % NZ
        gx[d, 0] = go(remote(gath.at[0, 0], gath.at[d, 0], gx_s.at[d, 0], gx_r.at[d, 0], at(e, 0, 0)))

    def swap(d):
        if d in BUNDLE_IN:
            gx[d, 0].wait_recv()
        else:
            for j in range(NX):
                if j or (d and d in DIRECT_IN):
                    gx[d, j].wait_recv()
        gc[d] = go(remote(gath.at[d, 0], gath.at[d, 1], gc_s.at[d], gc_r.at[d], at(0, 0, 1)))

    def transpose(k):
        loads[k].wait()
        textt[:, k * span : (k + 1) * span] = text[k * span : (k + 1) * span, :].T

    def repack(slot):
        d = SLOTS[slot]
        gc[d].wait_recv()
        for cr in range(2):
            for i in range(0, NX, 2):
                a = from_travel(gath[d, cr, i].astype(jnp.float32))
                b = from_travel(gath[d, cr, i + 1].astype(jnp.float32))
                r0 = slot * PLANE + cr * PAIR + i * OWN
                regs[r0 : r0 + 2 * OWN, :] = jnp.concatenate([a, b], axis=0).astype(jnp.bfloat16)

    top = {}

    def logits(g):
        lo = g * CHUNK
        peak = jnp.full((CHUNK, 128), -jnp.inf, jnp.float32)
        for t in range(VDEV // QTILE):
            dots = jnp.dot(
                regs[lo : lo + CHUNK, :], textt[:, t * QTILE : (t + 1) * QTILE],
                preferred_element_type=jnp.float32,
            )
            logit[g, :, t * QTILE : (t + 1) * QTILE] = dots
            for q in range(QTILE // 128):
                peak = jnp.maximum(peak, dots[:, q * 128 : (q + 1) * 128])
        top[g] = jnp.max(peak, axis=1, keepdims=True)

    def weights(g):
        lo = g * CHUNK
        total = jnp.zeros((CHUNK, 128), jnp.float32)
        for k in range(VDEV // 128):
            e = jnp.exp2((logit[g, :, k * 128 : (k + 1) * 128] - top[g]) * SCALE)
            total = total + e
            wgt[lo : lo + CHUNK, k * 128 : (k + 1) * 128] = e.astype(jnp.bfloat16)
        s = jnp.sum(total, axis=1, keepdims=True)
        pbuf[lo : lo + CHUNK, D:] = pack_ms(top[g], s)

    rc, rx, rz = {}, {}, {}

    def values(g):
        lo = g * CHUNK
        for k in range(2):
            pbuf[lo : lo + CHUNK, k * HALF : (k + 1) * HALF] = jnp.dot(
                wgt[lo : lo + CHUNK, :], text[:, k * HALF : (k + 1) * HALF], preferred_element_type=jnp.float32
            )
            if k == 0:
                give(g, 0)

    def give(g, k=1):
        cols = pl.ds(0, HALF) if k == 0 else pl.ds(HALF, WIDE - HALF)
        for slot in (2 * g + 1, 2 * g):
            rc[slot, k] = go(remote(
                pbuf.at[pl.ds(slot * PLANE + PAIR, PAIR), cols], cbuf.at[slot, :, cols],
                rc_s.at[slot, k], rc_r.at[slot, k], at(0, 0, 1),
            ))

    def pair_sum(slot):
        d = SLOTS[slot]
        rc[slot, 0].wait_recv()
        rc[slot, 1].wait_recv()
        lo = slot * PLANE
        m, s, p = merge([unpack(pbuf[lo : lo + PAIR, :]), unpack(cbuf[slot])])
        straight = d in DIRECT_OUT
        e = (NZ - d) % NZ if straight else d
        for i in (2, 1, 3, 0):
            j = (NX - i) % NX
            lo, hi = i * OWN, (i + 1) * OWN
            if i == 0 and not (straight and d):
                qown[slot, :, :D] = p[lo:hi]
                qown[slot, :, D:] = pack_ms(m[lo:hi], s[lo:hi])
                continue
            xsend[d, i] = to_message(m[lo:hi], s[lo:hi], p[lo:hi])
            rx[e, j] = go(remote(
                xsend.at[d, i], xb.at[e, j], rx_s.at[d, i], rx_r.at[e, j], at(d if straight else 0, i, 0)
            ))

    def plane(e, first):
        parts = list(first)
        for j in range(NX):
            if j or not first:
                rx[e, j].wait_recv()
                parts.append(from_message(xb[e, j]))
        return parts

    def x_sum(slot):
        d = SLOTS[slot]
        m, s, p = merge(plane(d, [unpack(qown[slot])]))
        zsend[d] = to_message(m, s, p)
        e = (NZ - d) % NZ
        rz[e] = go(remote(zsend.at[d], zb.at[e], rz_s.at[e], rz_r.at[e], at(d, 0, 0)))

    result = []

    def collect(e):
        if e == 0:
            parts = plane(0, [unpack(qown[0])])
        elif e in DIRECT_OUT:
            parts = plane(e, [])
        else:
            rz[e].wait_recv()
            parts = [from_message(zb[e])]
        result[:] = [merge(result + parts)]

    run = {
        "t": transpose, "fwd": forward, "bundle": bundle, "swap": swap, "pack": repack, "q": logits, "w": weights, "v": values,
        "give": give, "pair": pair_sum, "x": x_sum, "end": collect,
    }
    for e, i in SENDS:
        send(e, i)
    for name, k in STEPS:
        run[name](k)
    m, s, p = result[0]
    out_ref[...] = (p / s).astype(jnp.bfloat16)
    for cp in started:
        cp.wait_send()


def local(codes, exps, text_bank):
    dma = pltpu.SemaphoreType.DMA
    f32, bf16 = jnp.float32, jnp.bfloat16
    n = NZ * PLANE
    return pl.pallas_call(
        kernel,
        out_shape=jax.ShapeDtypeStruct((OWN, D), bf16),
        in_specs=[pl.BlockSpec(memory_space=pltpu.HBM)] * 3,
        out_specs=pl.BlockSpec(memory_space=pltpu.VMEM),
        scratch_shapes=[
            pltpu.VMEM((OWN, D), bf16),
            pltpu.VMEM((OWN, D // 32), jnp.int32),
            pltpu.VMEM((VDEV, D), bf16),
            pltpu.VMEM((D, VDEV), bf16),
            pltpu.VMEM((NZ, 2, NX, 2 * OWN, HALF), bf16),
            pltpu.VMEM((n, D), bf16),
            pltpu.VMEM((NCHUNK, CHUNK, VDEV), f32),
            pltpu.VMEM((n, VDEV), bf16),
            pltpu.VMEM((n, WIDE), f32),
            pltpu.VMEM((NZ, PAIR, WIDE), f32),
            pltpu.VMEM((NZ, NX, 2 * OWN, MSG), bf16),
            pltpu.VMEM((NZ, NX, 2 * OWN, MSG), bf16),
            pltpu.VMEM((NZ, OWN, WIDE), f32),
            pltpu.VMEM((NZ, 2 * OWN, MSG), bf16),
            pltpu.VMEM((NZ, 2 * OWN, MSG), bf16),
            dma((LOADS,)), dma((2,)),
            dma((NZ, NX)), dma((NZ, NX)),
            dma((NZ,)), dma((NZ,)),
            dma((NZ, 2)), dma((NZ, 2)),
            dma((NZ, NX)), dma((NZ, NX)),
            dma((NZ,)), dma((NZ,)),
        ],
        compiler_params=pltpu.CompilerParams(
            collective_id=0, has_side_effects=True, vmem_limit_bytes=56 * 2**20
        ),
    )(codes, exps, text_bank)


def solution(mesh):
    return jax.shard_map(
        local,
        mesh=mesh,
        in_specs=(P(("dp", "bank"), None), P(("dp", "bank"), None), P("bank", None)),
        out_specs=P(("dp", "bank"), None),
        check_vma=False,
    )
```

time: 51.1 us -> 44.7 us (0.87)
  Pallas kernels: 48.9 us -> 42.8 us
  local copies, waits for them, and re-layouts: 2.01 us -> 1.32 us
    pallas_call x1, Pallas kernels: 48.9 us -> 42.8 us  [local(): pl.pallas_call(kernel, out_shape=jax.ShapeDtypeStruct((OWN, D), bf16), in...]
    unnamed x5 -> x1, local copies, waits for them, and re-layouts: 2.01 us -> 1.32 us
where the time goes in v2:
time: 44.7 us; the launch traced here: 44.2 us
  Pallas kernels  42.8 us (96%)
  local copies, waits for them, and re-layouts  1.32 us (3%)
    pallas_call x1, Pallas kernels, local(): pl.pallas_call(kernel, out_shape=jax.ShapeDtypeStruct((OWN, D), bf16), in...  42.8 us
    unnamed x1, local copies, waits for them, and re-layouts  1.32 us

profile of v2, /device:TPU:16, one launch (start us, length us, event | category | flops | bytes accessed | tf_op | source)
XLA Modules:
  0.0 44.2 jit_solution(11563017185844087697)
XLA Ops:
  0.0 42.8 %shard_map.37 = bf16[8,1024]{1,0:T(8,128)(2,1)} custom-call(bf16[8,1024]{1,0:T(8,128)(2,1)} %codes_hbm.1, s32[8,32]{1,0:T(8,128)} %exps_hbm.1, bf16[4096,1024]{1,0:T(8,128)(2,1)} %text_hbm.1), custom_call_target="tpu_custom_call" | custom-call | tf_op jit(solution)/shard_map/pallas_call | solution.py:294
  42.9 1.3 %copy.5 = bf16[8,1024]{1,0:T(8,128)(2,1)} copy(bf16[8,1024]{1,0:T(8,128)(2,1)} %shard_map.37) | data formatting | bytes 32768

commit v3 on v2

--- a/solution.py
+++ b/solution.py
@@ -17,9 +17,9 @@
 PLANE = 2 * PAIR
 WIDE = D + 128
 MSG = HALF + 128
-SLOTS = (0, 1, 7, 2, 6, 3, 5, 4)
-CHUNK = 2 * PLANE
-NCHUNK = NZ // 2
+SLOTS = (0, 1, 7, 4, 3, 5, 2, 6)
+FIRST = ((0, 3), (3, 6), (6, 8))
+SECOND = ((0, 3), (3, 6), (6, 8))
 LOADS = 8
 QTILE = 512
 DIRECT_IN = (0, 1, 7)
@@ -31,13 +31,12 @@
 )
 STEPS = (
     ("t", 0), ("t", 1), ("t", 2), ("t", 3), ("t", 4), ("t", 5), ("t", 6), ("t", 7), ("swap", 0), ("bundle", 2),
-    ("bundle", 6), ("fwd", 3), ("fwd", 5), ("fwd", 4), ("swap", 1), ("swap", 7), ("pack", 0), ("pack", 1), ("q",
-    0), ("swap", 3), ("swap", 5), ("swap", 4), ("swap", 2), ("swap", 6), ("pack", 6), ("pack", 7), ("q", 3),
-    ("w", 0), ("pack", 4), ("pack", 5), ("q", 2), ("w", 3), ("v", 3), ("w", 2), ("give", 3), ("pack", 2),
-    ("pack", 3), ("q", 1), ("v", 2), ("w", 1), ("give", 2), ("pair", 7), ("pair", 6), ("v", 1), ("give", 1),
-    ("pair", 5), ("pair", 4), ("v", 0), ("give", 0), ("x", 7), ("x", 6), ("pair", 3), ("pair", 2), ("x", 5),
-    ("x", 4), ("pair", 1), ("pair", 0), ("x", 3), ("end", 0), ("end", 1), ("end", 7), ("end", 6), ("end", 2),
-    ("end", 3), ("end", 5), ("end", 4),
+    ("bundle", 6), ("fwd", 3), ("fwd", 5), ("fwd", 4), ("swap", 1), ("swap", 7), ("pack", 0), ("pack", 1),
+    ("pack", 2), ("q", 0), ("swap", 3), ("swap", 5), ("swap", 4), ("swap", 2), ("swap", 6), ("w", 0), ("va", 0),
+    ("vb", 0), ("pack", 3), ("pack", 4), ("pack", 5), ("q", 1), ("pair", 0), ("pair", 1), ("pair", 2), ("w", 1),
+    ("va", 1), ("vb", 1), ("pack", 6), ("pack", 7), ("q", 2), ("w", 2), ("va", 2), ("pair", 3), ("pair", 4),
+    ("pair", 5), ("vb", 2), ("end", 0), ("end", 1), ("end", 7), ("pair", 6), ("pair", 7), ("x", 3), ("x", 4),
+    ("x", 5), ("x", 6), ("x", 7), ("end", 3), ("end", 5), ("end", 4), ("end", 2), ("end", 6),
 )
 SCALE = 2.0 / math.log(2.0)
 
@@ -185,42 +184,35 @@
     top = {}
 
     def logits(g):
-        lo = g * CHUNK
-        peak = jnp.full((CHUNK, 128), -jnp.inf, jnp.float32)
+        lo, hi = FIRST[g][0] * PLANE, FIRST[g][1] * PLANE
+        peak = jnp.full((hi - lo, 128), -jnp.inf, jnp.float32)
         for t in range(VDEV // QTILE):
             dots = jnp.dot(
-                regs[lo : lo + CHUNK, :], textt[:, t * QTILE : (t + 1) * QTILE],
-                preferred_element_type=jnp.float32,
+                regs[lo:hi, :], textt[:, t * QTILE : (t + 1) * QTILE], preferred_element_type=jnp.float32
             )
-            logit[g, :, t * QTILE : (t + 1) * QTILE] = dots
+            logit[lo:hi, t * QTILE : (t + 1) * QTILE] = dots
             for q in range(QTILE // 128):
                 peak = jnp.maximum(peak, dots[:, q * 128 : (q + 1) * 128])
         top[g] = jnp.max(peak, axis=1, keepdims=True)
 
     def weights(g):
-        lo = g * CHUNK
-        total = jnp.zeros((CHUNK, 128), jnp.float32)
+        lo, hi = FIRST[g][0] * PLANE, FIRST[g][1] * PLANE
+        total = jnp.zeros((hi - lo, 128), jnp.float32)
         for k in range(VDEV // 128):
-            e = jnp.exp2((logit[g, :, k * 128 : (k + 1) * 128] - top[g]) * SCALE)
+            e = jnp.exp2((logit[lo:hi, k * 128 : (k + 1) * 128] - top[g]) * SCALE)
             total = total + e
-            wgt[lo : lo + CHUNK, k * 128 : (k + 1) * 128] = e.astype(jnp.bfloat16)
-        s = jnp.sum(total, axis=1, keepdims=True)
-        pbuf[lo : lo + CHUNK, D:] = pack_ms(top[g], s)
+            wgt[lo:hi, k * 128 : (k + 1) * 128] = e.astype(jnp.bfloat16)
+        pbuf[lo:hi, D:] = pack_ms(top[g], jnp.sum(total, axis=1, keepdims=True))
 
     rc, rx, rz = {}, {}, {}
 
-    def values(g):
-        lo = g * CHUNK
-        for k in range(2):
-            pbuf[lo : lo + CHUNK, k * HALF : (k + 1) * HALF] = jnp.dot(
-                wgt[lo : lo + CHUNK, :], text[:, k * HALF : (k + 1) * HALF], preferred_element_type=jnp.float32
-            )
-            if k == 0:
-                give(g, 0)
-
-    def give(g, k=1):
+    def values(h, k):
+        lo, hi = SECOND[h][0] * PLANE, SECOND[h][1] * PLANE
+        pbuf[lo:hi, k * HALF : (k + 1) * HALF] = jnp.dot(
+            wgt[lo:hi, :], text[:, k * HALF : (k + 1) * HALF], preferred_element_type=jnp.float32
+        )
         cols = pl.ds(0, HALF) if k == 0 else pl.ds(HALF, WIDE - HALF)
-        for slot in (2 * g + 1, 2 * g):
+        for slot in range(*SECOND[h]):
             rc[slot, k] = go(remote(
                 pbuf.at[pl.ds(slot * PLANE + PAIR, PAIR), cols], cbuf.at[slot, :, cols],
                 rc_s.at[slot, k], rc_r.at[slot, k], at(0, 0, 1),
@@ -274,8 +266,8 @@
         result[:] = [merge(result + parts)]
 
     run = {
-        "t": transpose, "fwd": forward, "bundle": bundle, "swap": swap, "pack": repack, "q": logits, "w": weights, "v": values,
-        "give": give, "pair": pair_sum, "x": x_sum, "end": collect,
+        "t": transpose, "fwd": forward, "bundle": bundle, "swap": swap, "pack": repack, "q": logits, "w": weights,
+        "va": lambda h: values(h, 0), "vb": lambda h: values(h, 1), "pair": pair_sum, "x": x_sum, "end": collect,
     }
     for e, i in SENDS:
         send(e, i)
@@ -303,7 +295,7 @@
             pltpu.VMEM((D, VDEV), bf16),
             pltpu.VMEM((NZ, 2, NX, 2 * OWN, HALF), bf16),
             pltpu.VMEM((n, D), bf16),
-            pltpu.VMEM((NCHUNK, CHUNK, VDEV), f32),
+            pltpu.VMEM((n, VDEV), f32),
             pltpu.VMEM((n, VDEV), bf16),
             pltpu.VMEM((n, WIDE), f32),
             pltpu.VMEM((NZ, PAIR, WIDE), f32),

time: 44.7 us -> 42.6 us (0.953)
  Pallas kernels: 42.8 us -> 40.4 us
    pallas_call x1, Pallas kernels: 42.8 us -> 40.4 us  [local(): pl.pallas_call(kernel, out_shape=jax.ShapeDtypeStruct((OWN, D), bf16), in...]
where the time goes in v3:
time: 42.6 us; the launch traced here: 41.8 us
  Pallas kernels  40.4 us (95%)
  local copies, waits for them, and re-layouts  1.32 us (3%)
    pallas_call x1, Pallas kernels, local(): pl.pallas_call(kernel, out_shape=jax.ShapeDtypeStruct((OWN, D), bf16), in...  40.4 us
    unnamed x1, local copies, waits for them, and re-layouts  1.32 us

profile of v3, /device:TPU:16, one launch (start us, length us, event | category | flops | bytes accessed | tf_op | source)
XLA Modules:
  0.0 41.8 jit_solution(1228391817227795839)
XLA Ops:
  0.0 40.4 %shard_map.37 = bf16[8,1024]{1,0:T(8,128)(2,1)} custom-call(bf16[8,1024]{1,0:T(8,128)(2,1)} %codes_hbm.1, s32[8,32]{1,0:T(8,128)} %exps_hbm.1, bf16[4096,1024]{1,0:T(8,128)(2,1)} %text_hbm.1), custom_call_target="tpu_custom_call" | custom-call | tf_op jit(solution)/shard_map/pallas_call | solution.py:286
  40.4 1.3 %copy.5 = bf16[8,1024]{1,0:T(8,128)(2,1)} copy(bf16[8,1024]{1,0:T(8,128)(2,1)} %shard_map.37) | data formatting | bytes 32768

commit v4 on v3

--- a/solution.py
+++ b/solution.py
@@ -30,8 +30,8 @@
     0),
 )
 STEPS = (
-    ("t", 0), ("t", 1), ("t", 2), ("t", 3), ("t", 4), ("t", 5), ("t", 6), ("t", 7), ("swap", 0), ("bundle", 2),
-    ("bundle", 6), ("fwd", 3), ("fwd", 5), ("fwd", 4), ("swap", 1), ("swap", 7), ("pack", 0), ("pack", 1),
+    ("t", 0), ("t", 1), ("t", 2), ("swap", 0), ("bundle", 2), ("bundle", 6), ("fwd", 3), ("fwd", 5), ("t", 3),
+    ("fwd", 4), ("swap", 1), ("swap", 7), ("t", 4), ("t", 5), ("t", 6), ("t", 7), ("pack", 0), ("pack", 1),
     ("pack", 2), ("q", 0), ("swap", 3), ("swap", 5), ("swap", 4), ("swap", 2), ("swap", 6), ("w", 0), ("va", 0),
     ("vb", 0), ("pack", 3), ("pack", 4), ("pack", 5), ("q", 1), ("pair", 0), ("pair", 1), ("pair", 2), ("w", 1),
     ("va", 1), ("vb", 1), ("pack", 6), ("pack", 7), ("q", 2), ("w", 2), ("va", 2), ("pair", 3), ("pair", 4),

time: 42.6 us -> 42 us (0.986); the launches traced: 41.8 us -> 41.8 us
  no operation moved by 1% of the time
where the time goes in v4:
time: 42 us; the launch traced here: 41.8 us
  Pallas kernels  40.5 us (96%)
  local copies, waits for them, and re-layouts  1.32 us (3%)
    pallas_call x1, Pallas kernels, local(): pl.pallas_call(kernel, out_shape=jax.ShapeDtypeStruct((OWN, D), bf16), in...  40.5 us
    unnamed x1, local copies, waits for them, and re-layouts  1.32 us

profile of v4, /device:TPU:16, one launch (start us, length us, event | category | flops | bytes accessed | tf_op | source)
XLA Modules:
  0.0 41.8 jit_solution(2246350572625764709)
XLA Ops:
  0.0 40.5 %shard_map.37 = bf16[8,1024]{1,0:T(8,128)(2,1)} custom-call(bf16[8,1024]{1,0:T(8,128)(2,1)} %codes_hbm.1, s32[8,32]{1,0:T(8,128)} %exps_hbm.1, bf16[4096,1024]{1,0:T(8,128)(2,1)} %text_hbm.1), custom_call_target="tpu_custom_call" | custom-call | tf_op jit(solution)/shard_map/pallas_call | solution.py:286
  40.5 1.3 %copy.5 = bf16[8,1024]{1,0:T(8,128)(2,1)} copy(bf16[8,1024]{1,0:T(8,128)(2,1)} %shard_map.37) | data formatting | bytes 32768

commit v5 on v4

--- a/solution.py
+++ b/solution.py
@@ -35,8 +35,8 @@
     ("pack", 2), ("q", 0), ("swap", 3), ("swap", 5), ("swap", 4), ("swap", 2), ("swap", 6), ("w", 0), ("va", 0),
     ("vb", 0), ("pack", 3), ("pack", 4), ("pack", 5), ("q", 1), ("pair", 0), ("pair", 1), ("pair", 2), ("w", 1),
     ("va", 1), ("vb", 1), ("pack", 6), ("pack", 7), ("q", 2), ("w", 2), ("va", 2), ("pair", 3), ("pair", 4),
-    ("pair", 5), ("vb", 2), ("end", 0), ("end", 1), ("end", 7), ("pair", 6), ("pair", 7), ("x", 3), ("x", 4),
-    ("x", 5), ("x", 6), ("x", 7), ("end", 3), ("end", 5), ("end", 4), ("end", 2), ("end", 6),
+    ("pair", 5), ("vb", 2), ("end", 0), ("end", 1), ("end", 7), ("sent", 11), ("pair", 6), ("pair", 7), ("x", 3), ("x", 4),
+    ("x", 5), ("x", 6), ("x", 7), ("sent", 5), ("end", 3), ("end", 5), ("end", 4), ("end", 2), ("end", 6),
 )
 SCALE = 2.0 / math.log(2.0)
 
@@ -265,8 +265,13 @@
             parts = [from_message(zb[e])]
         result[:] = [merge(result + parts)]
 
+    def drain(keep):
+        for copy in started[: len(started) - keep]:
+            copy.wait_send()
+        del started[: len(started) - keep]
+
     run = {
-        "t": transpose, "fwd": forward, "bundle": bundle, "swap": swap, "pack": repack, "q": logits, "w": weights,
+        "sent": drain, "t": transpose, "fwd": forward, "bundle": bundle, "swap": swap, "pack": repack, "q": logits, "w": weights,
         "va": lambda h: values(h, 0), "vb": lambda h: values(h, 1), "pair": pair_sum, "x": x_sum, "end": collect,
     }
     for e, i in SENDS:

time: 42 us -> 41.9 us (level)
  no operation moved by 1% of the time
where the time goes in v5:
time: 41.9 us; the launch traced here: 41.7 us
  Pallas kernels  40.4 us (96%)
  local copies, waits for them, and re-layouts  1.32 us (3%)
    pallas_call x1, Pallas kernels, local(): pl.pallas_call(kernel, out_shape=jax.ShapeDtypeStruct((OWN, D), bf16), in...  40.4 us
    unnamed x1, local copies, waits for them, and re-layouts  1.32 us

profile of v5, /device:TPU:16, one launch (start us, length us, event | category | flops | bytes accessed | tf_op | source)
XLA Modules:
  0.0 41.7 jit_solution(1980291498796931161)
XLA Ops:
  0.0 40.4 %shard_map.37 = bf16[8,1024]{1,0:T(8,128)(2,1)} custom-call(bf16[8,1024]{1,0:T(8,128)(2,1)} %codes_hbm.1, s32[8,32]{1,0:T(8,128)} %exps_hbm.1, bf16[4096,1024]{1,0:T(8,128)(2,1)} %text_hbm.1), custom_call_target="tpu_custom_call" | custom-call | tf_op jit(solution)/shard_map/pallas_call | solution.py:291
  40.4 1.3 %copy.5 = bf16[8,1024]{1,0:T(8,128)(2,1)} copy(bf16[8,1024]{1,0:T(8,128)(2,1)} %shard_map.37) | data formatting | bytes 32768
